TPU v7x, 128 devices: a whole 4x4x4 slice. The times are simulated.
128 devices in a mesh: gx: 8 (over x, core), gy: 16 (over y, z).
Axes of the slice: x: 4, y: 4, z: 4, core: 2. Of those that a mesh axis runs over, the one named last changes fastest.
Arguments:
- psi: float32 [2, 2, 160, 320, 128], P(None, None, 'gx', 'gy'), may hold values from -18 to 18
- basis: float32 [2, 8, 160, 320, 128], P(None, None, 'gx', 'gy'), may hold values from -81 to 81
- potential: float32 [160, 320, 128], P('gx', 'gy'), may hold values from -3 to 1
Outputs:
- psi_half: float32 [2, 2, 160, 320, 128], P(None, None, 'gx', 'gy')
All inputs are finite; a program needn't handle non-finite values.
Results may differ from a plain program's by a relative error of at most 0.003.
Values sent between devices are 32-bit elements; how exact they have to be, the bound alone decides.
A program may use at most 192 MiB of HBM per device.

v0:
```python
import jax
import jax.numpy as jnp
from jax import lax
from jax.sharding import PartitionSpec as P

coefficients = [
    -5369.0 / 1800.0,
    12.0 / 7.0,
    -15.0 / 56.0,
    10.0 / 189.0,
    -1.0 / 112.0,
    2.0 / 1925.0,
    -1.0 / 16632.0,
]
step_size = 0.25


def padded_2(block, sides, width):
    for axis, dim in sides:
        count = lax.axis_size(axis)
        forward = [(i, i + 1) for i in range(count - 1)]
        forward.append((count - 1, 0))
        backward = [(target, source) for source, target in forward]
        low = lax.ppermute(
            lax.slice_in_dim(block, block.shape[dim] - width, None, axis=dim), axis, forward
        )
        high = lax.ppermute(lax.slice_in_dim(block, 0, width, axis=dim), axis, backward)
        block = jnp.concatenate([low, block, high], axis=dim)
    return block


def laplace(padded):
    width_x = padded.shape[2] - 12
    width_y = padded.shape[3] - 12
    center = padded[:, :, 6 : 6 + width_x, 6 : 6 + width_y, :]
    total = 3.0 * coefficients[0] * center
    for offset in range(1, 7):
        near = padded[:, :, 6 + offset : 6 + offset + width_x, 6 : 6 + width_y, :]
        near = near + padded[:, :, 6 - offset : 6 - offset + width_x, 6 : 6 + width_y, :]
        near = near + padded[:, :, 6 : 6 + width_x, 6 + offset : 6 + offset + width_y, :]
        near = near + padded[:, :, 6 : 6 + width_x, 6 - offset : 6 - offset + width_y, :]
        near = near + jnp.roll(center, offset, axis=4) + jnp.roll(center, -offset, axis=4)
        total = total + coefficients[offset] * near
    return (total, center)


def intersections(field, basis, ncell):
    count = basis.shape[1]
    flat_field = field.reshape(4, -1)
    flat_basis = basis.reshape(2 * count, -1)
    cross = lax.dot_general(
        flat_basis, flat_field, (((1,), (1,)), ((), ())), precision=lax.Precision.HIGHEST
    )
    cross = lax.psum(cross, ("gx", "gy")) / ncell
    parts = cross.reshape(2, count, 2, 2)
    real_part = parts[0, :, :, 0] + parts[1, :, :, 1]
    imag_part = parts[0, :, :, 1] - parts[1, :, :, 0]
    return (real_part, imag_part)


def hamiltonian(padded, potential, basis, real_part, imag_part):
    lap_term, center = laplace(padded)
    kinetic = -0.5 * lap_term + potential[None, None] * center
    high = lax.Precision.HIGHEST
    corr_real = jnp.einsum("kxyz,kj->jxyz", basis[0], real_part, precision=high) - jnp.einsum(
        "kxyz,kj->jxyz", basis[1], imag_part, precision=high
    )
    corr_imag = jnp.einsum("kxyz,kj->jxyz", basis[0], imag_part, precision=high) + jnp.einsum(
        "kxyz,kj->jxyz", basis[1], real_part, precision=high
    )
    return jnp.stack([kinetic[:, 0] - corr_real, kinetic[:, 1] - corr_imag], 1)


def advance(applied, term_index):
    factor = step_size / term_index
    return jnp.stack([factor * applied[:, 1], -factor * applied[:, 0]], 1)


def per_device(psi, basis, potential):
    ncell = psi.shape[2] * lax.axis_size("gx") * psi.shape[3] * lax.axis_size("gy") * psi.shape[4]
    term = psi
    result = psi
    for term_index in range(1, 5):
        padded = padded_2(term, (("gx", 2), ("gy", 3)), 6)
        real_part, imag_part = intersections(term, basis, ncell)
        applied = hamiltonian(padded, potential, basis, real_part, imag_part)
        term = advance(applied, term_index)
        result = result + term
    return result


def solution(mesh):
    placed = (P(None, None, "gx", "gy", None), P(None, None, "gx", "gy", None), P("gx", "gy", None))
    return jax.shard_map(
        per_device,
        mesh=mesh,
        in_specs=placed,
        out_specs=P(None, None, "gx", "gy", None),
        check_vma=False,
    )
```

profile of v0, /device:TPU:1, one launch (start us, length us, event | category | flops | bytes accessed | tf_op | source)
XLA Modules:
  0.0 637.3 jit_solution(6755122577008997523)
XLA Ops:
  2.0 2.6 collective-permute-start.1
  30.2 18.5 %fusion.342 = f32[16,4]{0,1:T(4,128)S(1)} fusion(f32[16,51200]{1,0:T(8,128)} %bitcast.225, f32[4,51200]{1,0:T(4,128)S(1)} %reshape.48), kind=kOutput, calls=%fused_computation.578 | convolution fusion | flops 39321600 | bytes 4096256 | tf_op jit(solution)/shard_map/dot_general | solution.py:51
  48.7 67.2 %psum.28 = f32[16,4]{0,1:T(4,128)S(1)} all-reduce(f32[16,4]{0,1:T(4,128)S(1)} %fusion.342), channel_id=1, replica_groups=mesh['gx'=8,'gy'=16] {'gx','gy'}, use_global_device_ids=true, to_apply=%region_0.0 | all-reduce | flops 64 | bytes 512 | tf_op jit(solution)/shard_map/psum | solution.py:54
  141.1 23.6 %multiply_add_fusion.3 = f32[2,2,20,20,128]{4,0,3,2,1:T(2,128)S(1)} fusion(f32[2,2,20,20,6]{4,0,3,2,1:T(2,128)S(1)} %copy.87, f32[2,2,20,20,122]{4,0,3,2,1:T(2,128)S(1)} %copy.88, f32[2,2,20,20,122]{4,0,3,2,1:T(2,128)S(1)} %copy.89, f32[2,2,20,20,6]{4,0,3,2,1:T(2,128)S(1)} %copy.90, f32[2,2,32,20,128]{4,0,3,2,1:T(2,128)S(1)} %get-tuple-element.133, ...), kind=kLoop, calls=%fused_computation.518 | loop fusion | flops 14336000 | bytes 23601152 | tf_op jit(solution)/shard_map/add | solution.py:63
  183.5 2.6 fusion.235
  199.1 6.2 convolution_bitcast_fusion.2
  205.3 66.4 %psum.29 = f32[16,4]{0,1:T(4,128)S(1)} all-reduce(f32[16,4]{0,1:T(4,128)S(1)} %convolution_bitcast_fusion.2), channel_id=1, replica_groups=mesh['gx'=8,'gy'=16] {'gx','gy'}, use_global_device_ids=true, to_apply=%region_1.2 | all-reduce | flops 64 | bytes 512 | tf_op jit(solution)/shard_map/psum | solution.py:54
  271.9 3.0 fusion.10
  274.9 3.0 fusion.8
  283.1 5.4 collective-permute-done.6
  288.5 5.2 collective-permute-done.7
  293.7 4.1 pad_maximum_fusion
  298.1 18.9 %multiply_add_fusion.2 = f32[2,2,20,20,128]{4,0,3,2,1:T(2,128)S(1)} fusion(f32[2,2,20,20,6]{4,0,3,2,1:T(2,128)S(1)} %get-tuple-element.100, f32[2,2,20,20,122]{4,0,3,2,1:T(2,128)S(1)} %copy-done.91, f32[2,2,20,20,122]{4,0,3,2,1:T(2,128)S(1)} %copy-done.90, f32[2,2,20,20,6]{4,0,3,2,1:T(2,128)S(1)} %get-tuple-element.99, ...), kind=kLoop, calls=%fused_computation.517 | loop fusion | flops 12083200 | bytes 31334400 | tf_op jit(solution)/shard_map/add | solution.py:63
  334.7 2.6 fusion.211
  351.6 6.2 convolution_bitcast_fusion.1
  357.7 64.5 %psum.30 = f32[16,4]{0,1:T(4,128)S(1)} all-reduce(f32[16,4]{0,1:T(4,128)S(1)} %convolution_bitcast_fusion.1), channel_id=1, replica_groups=mesh['gx'=8,'gy'=16] {'gx','gy'}, use_global_device_ids=true, to_apply=%region_2.3 | all-reduce | flops 64 | bytes 512 | tf_op jit(solution)/shard_map/psum | solution.py:54
  422.4 3.0 fusion.6
  425.4 3.0 fusion.4
  435.8 4.3 collective-permute-done.10
  440.1 5.2 collective-permute-done.11
  445.3 6.5 %pad_maximum_fusion.1 = (f32[2,2,32,26,128]{4,0,3,2,1:T(2,128)S(1)}, f32[2,2,32,26,128]{4,0,3,2,1:T(2,128)S(1)}) fusion(f32[2,2,32,6,128]{4,0,3,2,1:T(2,128)S(1)} %collective-permute-done.10, f32[2,2,6,20,128]{4,0,3,2,1:T(2,128)} %collective-permute-done.8, f32[2,1,20,20,128]{4,0,3,2,1:T(2,128)S(1)} %fusion.77, f32[2,1,20,20,128]{4,0,3,2,1:T(2,128)S(1)} %fusion.65, ...), kind=kLoop, calls=%fused_computation.12 | loop fusion | flops 3407872 | bytes 5505024 | tf_op jit(solution)/shard_map/concatenate | solution.py:28
  452.1 18.9 %multiply_add_fusion.1 = f32[2,2,20,20,128]{4,0,3,2,1:T(2,128)S(1)} fusion(f32[2,2,20,20,6]{4,0,3,2,1:T(2,128)S(1)} %get-tuple-element.72, f32[2,2,20,20,122]{4,0,3,2,1:T(2,128)S(1)} %copy-done.93, f32[2,2,20,20,122]{4,0,3,2,1:T(2,128)S(1)} %copy-done.92, f32[2,2,20,20,6]{4,0,3,2,1:T(2,128)S(1)} %get-tuple-element.71, ...), kind=kLoop, calls=%fused_computation.516 | loop fusion | flops 12083200 | bytes 31334400 | tf_op jit(solution)/shard_map/add | solution.py:63
  488.9 2.6 fusion.187
  505.4 2.5 reshape.54
  507.8 6.1 convolution_bitcast_fusion
  514.0 64.5 %psum.31 = f32[16,4]{0,1:T(4,128)S(1)} all-reduce(f32[16,4]{0,1:T(4,128)S(1)} %convolution_bitcast_fusion), channel_id=1, replica_groups=mesh['gx'=8,'gy'=16] {'gx','gy'}, use_global_device_ids=true, to_apply=%region_3.4 | all-reduce | flops 64 | bytes 512 | tf_op jit(solution)/shard_map/psum | solution.py:54
  578.6 3.0 fusion.2
  581.6 3.0 fusion
  592.2 4.1 collective-permute-done.14
  596.3 5.2 collective-permute-done.15
  601.5 6.5 %pad_maximum_fusion.2 = (f32[2,2,32,26,128]{4,0,3,2,1:T(2,128)S(1)}, f32[2,2,32,26,128]{4,0,3,2,1:T(2,128)S(1)}) fusion(f32[2,2,32,6,128]{4,0,3,2,1:T(2,128)S(1)} %collective-permute-done.14, f32[2,2,6,20,128]{4,0,3,2,1:T(2,128)} %collective-permute-done.12, f32[2,1,20,20,128]{4,0,3,2,1:T(2,128)S(1)} %fusion.101, f32[2,1,20,20,128]{4,0,3,2,1:T(2,128)S(1)} %fusion.89, ...), kind=kLoop, calls=%fused_computation.14 | loop fusion | flops 3407872 | bytes 5505024 | tf_op jit(solution)/shard_map/concatenate | solution.py:28
  608.3 22.5 %multiply_add_fusion = f32[2,2,20,20,128]{4,0,3,2,1:T(2,128)S(1)} fusion(f32[2,2,20,20,6]{4,0,3,2,1:T(2,128)S(1)} %get-tuple-element.44, f32[2,2,20,20,122]{4,0,3,2,1:T(2,128)} %get-tuple-element.46, f32[2,2,20,20,122]{4,0,3,2,1:T(2,128)S(1)} %copy-done.94, f32[2,2,20,20,6]{4,0,3,2,1:T(2,128)S(1)} %get-tuple-element.43, ...), kind=kLoop, calls=%fused_computation.515 | loop fusion | flops 12083200 | bytes 31334400 | tf_op jit(solution)/shard_map/add | solution.py:63
  (334 shorter events, 174.1 us)
Async XLA Ops:
  2.0 114.0 %collective-permute-start.1 = (f32[2,2,6,20,128]{4,0,3,2,1:T(2,128)}, f32[2,2,6,20,128]{4,0,3,2,1:T(2,128)}, u32[]{:S(2)}, u32[]{:S(2)}) collective-permute-start(f32[2,2,6,20,128]{4,0,3,2,1:T(2,128)} %copy.91), channel_id=1, source_target_pairs={{0,16},{16,32},{32,48},{48,64},{64,80},{80,96},{96,112},{112,0},{1... | collective-permute-start | bytes 737288 | tf_op jit(solution)/shard_map/ppermute | solution.py:24
  5.4 112.8 %collective-permute-start = (f32[2,2,6,20,128]{4,0,3,2,1:T(2,128)}, f32[2,2,6,20,128]{4,0,3,2,1:T(2,128)}, u32[]{:S(2)}, u32[]{:S(2)}) collective-permute-start(f32[2,2,6,20,128]{4,0,3,2,1:T(2,128)} %copy.92), channel_id=1, source_target_pairs={{16,0},{32,16},{48,32},{64,48},{80,64},{96,80},{112,96},{0,112},{1... | collective-permute-start | bytes 737288 | tf_op jit(solution)/shard_map/ppermute | solution.py:27
  119.5 21.6 %collective-permute-start.2 = (f32[2,2,32,6,128]{4,0,3,2,1:T(2,128)S(1)}, f32[2,2,32,6,128]{4,0,3,2,1:T(2,128)S(1)}, u32[]{:S(2)}, u32[]{:S(2)}) collective-permute-start(f32[2,2,32,6,128]{4,0,3,2,1:T(2,128)S(1)} %get-tuple-element.17), channel_id=1, source_target_pairs={{1,0},{2,1},{3,2},{4,3},{5,4},{6,5},{7,6},{8,7},{9,8},{10,9},{11,1... | collective-permute-start | bytes 1179656 | tf_op jit(solution)/shard_map/ppermute | solution.py:27
  121.9 19.2 %collective-permute-start.3 = (f32[2,2,32,6,128]{4,0,3,2,1:T(2,128)S(1)}, f32[2,2,32,6,128]{4,0,3,2,1:T(2,128)S(1)}, u32[]{:S(2)}, u32[]{:S(2)}) collective-permute-start(f32[2,2,32,6,128]{4,0,3,2,1:T(2,128)S(1)} %get-tuple-element.18), channel_id=1, source_target_pairs={{0,1},{1,2},{2,3},{3,4},{4,5},{5,6},{6,7},{7,8},{8,9},{9,10},{10,1... | collective-permute-start | bytes 1179656 | tf_op jit(solution)/shard_map/ppermute | solution.py:24
  196.0 81.9 %collective-permute-start.4 = (f32[2,2,6,20,128]{4,0,3,2,1:T(2,128)}, f32[2,2,6,20,128]{4,0,3,2,1:T(2,128)S(1)}, u32[]{:S(2)}, u32[]{:S(2)}) collective-permute-start(f32[2,2,6,20,128]{4,0,3,2,1:T(2,128)} %get-tuple-element.98), channel_id=1, source_target_pairs={{16,0},{32,16},{48,32},{64,48},{80,64},{96,80},{112,96},{0,112},{1... | collective-permute-start | bytes 737288 | tf_op jit(solution)/shard_map/ppermute | solution.py:27
  197.0 80.9 %collective-permute-start.5 = (f32[2,2,6,20,128]{4,0,3,2,1:T(2,128)}, f32[2,2,6,20,128]{4,0,3,2,1:T(2,128)S(1)}, u32[]{:S(2)}, u32[]{:S(2)}) collective-permute-start(f32[2,2,6,20,128]{4,0,3,2,1:T(2,128)} %get-tuple-element.97), channel_id=1, source_target_pairs={{0,16},{16,32},{32,48},{48,64},{64,80},{80,96},{96,112},{112,0},{1... | collective-permute-start | bytes 737288 | tf_op jit(solution)/shard_map/ppermute | solution.py:24
  199.1 98.7 %copy-start.91 = (f32[2,2,20,20,122]{4,0,3,2,1:T(2,128)S(1)}, f32[2,2,20,20,122]{4,0,3,2,1:T(2,128)}, u32[]{:S(2)}) copy-start(f32[2,2,20,20,122]{4,0,3,2,1:T(2,128)} %get-tuple-element.102) | copy-start | bytes 2342404
  271.9 26.0 %copy-start.89 = (f32[2,2,20,20,5]{4,0,3,2,1:T(2,128)S(1)}, f32[2,2,20,20,5]{4,0,3,2,1:T(2,128)}, u32[]{:S(2)}) copy-start(f32[2,2,20,20,5]{4,0,3,2,1:T(2,128)} %get-tuple-element.92) | copy-start | bytes 96004
  271.9 26.0 %copy-start.90 = (f32[2,2,20,20,122]{4,0,3,2,1:T(2,128)S(1)}, f32[2,2,20,20,122]{4,0,3,2,1:T(2,128)}, u32[]{:S(2)}) copy-start(f32[2,2,20,20,122]{4,0,3,2,1:T(2,128)} %get-tuple-element.101) | copy-start | bytes 2342404
  278.4 10.1 %collective-permute-start.6 = (f32[2,2,32,6,128]{4,0,3,2,1:T(2,128)S(1)}, f32[2,2,32,6,128]{4,0,3,2,1:T(2,128)S(1)}, u32[]{:S(2)}, u32[]{:S(2)}) collective-permute-start(f32[2,2,32,6,128]{4,0,3,2,1:T(2,128)S(1)} %get-tuple-element.15), channel_id=1, source_target_pairs={{1,0},{2,1},{3,2},{4,3},{5,4},{6,5},{7,6},{8,7},{9,8},{10,9},{11,1... | collective-permute-start | bytes 1179656 | tf_op jit(solution)/shard_map/ppermute | solution.py:27
  280.8 12.9 %collective-permute-start.7 = (f32[2,2,32,6,128]{4,0,3,2,1:T(2,128)S(1)}, f32[2,2,32,6,128]{4,0,3,2,1:T(2,128)S(1)}, u32[]{:S(2)}, u32[]{:S(2)}) collective-permute-start(f32[2,2,32,6,128]{4,0,3,2,1:T(2,128)S(1)} %get-tuple-element.16), channel_id=1, source_target_pairs={{0,1},{1,2},{2,3},{3,4},{4,5},{5,6},{6,7},{7,8},{8,9},{9,10},{10,1... | collective-permute-start | bytes 1179656 | tf_op jit(solution)/shard_map/ppermute | solution.py:24
  348.3 80.1 %collective-permute-start.8 = (f32[2,2,6,20,128]{4,0,3,2,1:T(2,128)}, f32[2,2,6,20,128]{4,0,3,2,1:T(2,128)}, u32[]{:S(2)}, u32[]{:S(2)}) collective-permute-start(f32[2,2,6,20,128]{4,0,3,2,1:T(2,128)} %get-tuple-element.70), channel_id=1, source_target_pairs={{16,0},{32,16},{48,32},{64,48},{80,64},{96,80},{112,96},{0,112},{1... | collective-permute-start | bytes 737288 | tf_op jit(solution)/shard_map/ppermute | solution.py:27
  350.2 78.2 %collective-permute-start.9 = (f32[2,2,6,20,128]{4,0,3,2,1:T(2,128)}, f32[2,2,6,20,128]{4,0,3,2,1:T(2,128)}, u32[]{:S(2)}, u32[]{:S(2)}) collective-permute-start(f32[2,2,6,20,128]{4,0,3,2,1:T(2,128)} %get-tuple-element.69), channel_id=1, source_target_pairs={{0,16},{16,32},{32,48},{48,64},{64,80},{80,96},{96,112},{112,0},{1... | collective-permute-start | bytes 737288 | tf_op jit(solution)/shard_map/ppermute | solution.py:24
  351.5 100.3 %copy-start.93 = (f32[2,2,20,20,122]{4,0,3,2,1:T(2,128)S(1)}, f32[2,2,20,20,122]{4,0,3,2,1:T(2,128)}, u32[]{:S(2)}) copy-start(f32[2,2,20,20,122]{4,0,3,2,1:T(2,128)} %get-tuple-element.74) | copy-start | bytes 2342404
  422.4 29.5 %copy-start.80 = (f32[2,2,20,20,5]{4,0,3,2,1:T(2,128)S(1)}, f32[2,2,20,20,5]{4,0,3,2,1:T(2,128)}, u32[]{:S(2)}) copy-start(f32[2,2,20,20,5]{4,0,3,2,1:T(2,128)} %get-tuple-element.63) | copy-start | bytes 96004
  422.4 29.5 %copy-start.81 = (f32[2,2,20,20,5]{4,0,3,2,1:T(2,128)S(1)}, f32[2,2,20,20,5]{4,0,3,2,1:T(2,128)}, u32[]{:S(2)}) copy-start(f32[2,2,20,20,5]{4,0,3,2,1:T(2,128)} %get-tuple-element.64) | copy-start | bytes 96004
  422.4 29.5 %copy-start.92 = (f32[2,2,20,20,122]{4,0,3,2,1:T(2,128)S(1)}, f32[2,2,20,20,122]{4,0,3,2,1:T(2,128)}, u32[]{:S(2)}) copy-start(f32[2,2,20,20,122]{4,0,3,2,1:T(2,128)} %get-tuple-element.73) | copy-start | bytes 2342404
  425.4 26.5 %copy-start.74 = (f32[2,2,20,20,123]{4,0,3,2,1:T(2,128)S(1)}, f32[2,2,20,20,123]{4,0,3,2,1:T(2,128)}, u32[]{:S(2)}) copy-start(f32[2,2,20,20,123]{4,0,3,2,1:T(2,128)} %get-tuple-element.65) | copy-start | bytes 2361604
  425.4 26.5 %copy-start.75 = (f32[2,2,20,20,123]{4,0,3,2,1:T(2,128)S(1)}, f32[2,2,20,20,123]{4,0,3,2,1:T(2,128)}, u32[]{:S(2)}) copy-start(f32[2,2,20,20,123]{4,0,3,2,1:T(2,128)} %get-tuple-element.66) | copy-start | bytes 2361604
  428.4 23.5 %copy-start.63 = (f32[2,2,20,20,124]{4,0,3,2,1:T(2,128)S(1)}, f32[2,2,20,20,124]{4,0,3,2,1:T(2,128)}, u32[]{:S(2)}) copy-start(f32[2,2,20,20,124]{4,0,3,2,1:T(2,128)} %get-tuple-element.62) | copy-start | bytes 2380804
  428.4 23.5 %copy-start.68 = (f32[2,2,20,20,4]{4,0,3,2,1:T(2,128)S(1)}, f32[2,2,20,20,4]{4,0,3,2,1:T(2,128)}, u32[]{:S(2)}) copy-start(f32[2,2,20,20,4]{4,0,3,2,1:T(2,128)} %get-tuple-element.59) | copy-start | bytes 76804
  430.0 10.1 %collective-permute-start.10 = (f32[2,2,32,6,128]{4,0,3,2,1:T(2,128)S(1)}, f32[2,2,32,6,128]{4,0,3,2,1:T(2,128)S(1)}, u32[]{:S(2)}, u32[]{:S(2)}) collective-permute-start(f32[2,2,32,6,128]{4,0,3,2,1:T(2,128)S(1)} %get-tuple-element.11), channel_id=1, source_target_pairs={{1,0},{2,1},{3,2},{4,3},{5,4},{6,5},{7,6},{8,7},{9,8},{10,9},{11,1... | collective-permute-start | bytes 1179656 | tf_op jit(solution)/shard_map/ppermute | solution.py:27
  432.4 13.0 %collective-permute-start.11 = (f32[2,2,32,6,128]{4,0,3,2,1:T(2,128)S(1)}, f32[2,2,32,6,128]{4,0,3,2,1:T(2,128)S(1)}, u32[]{:S(2)}, u32[]{:S(2)}) collective-permute-start(f32[2,2,32,6,128]{4,0,3,2,1:T(2,128)S(1)} %get-tuple-element.12), channel_id=1, source_target_pairs={{0,1},{1,2},{2,3},{3,4},{4,5},{5,6},{6,7},{7,8},{8,9},{9,10},{10,1... | collective-permute-start | bytes 1179656 | tf_op jit(solution)/shard_map/ppermute | solution.py:24
  502.4 82.2 %collective-permute-start.12 = (f32[2,2,6,20,128]{4,0,3,2,1:T(2,128)}, f32[2,2,6,20,128]{4,0,3,2,1:T(2,128)}, u32[]{:S(2)}, u32[]{:S(2)}) collective-permute-start(f32[2,2,6,20,128]{4,0,3,2,1:T(2,128)} %get-tuple-element.42), channel_id=1, source_target_pairs={{16,0},{32,16},{48,32},{64,48},{80,64},{96,80},{112,96},{0,112},{1... | collective-permute-start | bytes 737288 | tf_op jit(solution)/shard_map/ppermute | solution.py:27
  504.3 80.3 %collective-permute-start.13 = (f32[2,2,6,20,128]{4,0,3,2,1:T(2,128)}, f32[2,2,6,20,128]{4,0,3,2,1:T(2,128)}, u32[]{:S(2)}, u32[]{:S(2)}) collective-permute-start(f32[2,2,6,20,128]{4,0,3,2,1:T(2,128)} %get-tuple-element.41), channel_id=1, source_target_pairs={{0,16},{16,32},{32,48},{48,64},{64,80},{80,96},{96,112},{112,0},{1... | collective-permute-start | bytes 737288 | tf_op jit(solution)/shard_map/ppermute | solution.py:24
  578.6 29.5 %copy-start.83 = (f32[2,2,20,20,5]{4,0,3,2,1:T(2,128)S(1)}, f32[2,2,20,20,5]{4,0,3,2,1:T(2,128)}, u32[]{:S(2)}) copy-start(f32[2,2,20,20,5]{4,0,3,2,1:T(2,128)} %get-tuple-element.36) | copy-start | bytes 96004
  578.6 29.5 %copy-start.94 = (f32[2,2,20,20,122]{4,0,3,2,1:T(2,128)S(1)}, f32[2,2,20,20,122]{4,0,3,2,1:T(2,128)}, u32[]{:S(2)}) copy-start(f32[2,2,20,20,122]{4,0,3,2,1:T(2,128)} %get-tuple-element.45) | copy-start | bytes 2342404
  581.6 26.5 %copy-start.76 = (f32[2,2,20,20,123]{4,0,3,2,1:T(2,128)S(1)}, f32[2,2,20,20,123]{4,0,3,2,1:T(2,128)}, u32[]{:S(2)}) copy-start(f32[2,2,20,20,123]{4,0,3,2,1:T(2,128)} %get-tuple-element.37) | copy-start | bytes 2361604
  581.6 26.5 %copy-start.77 = (f32[2,2,20,20,123]{4,0,3,2,1:T(2,128)S(1)}, f32[2,2,20,20,123]{4,0,3,2,1:T(2,128)}, u32[]{:S(2)}) copy-start(f32[2,2,20,20,123]{4,0,3,2,1:T(2,128)} %get-tuple-element.38) | copy-start | bytes 2361604
  581.6 26.5 %copy-start.82 = (f32[2,2,20,20,5]{4,0,3,2,1:T(2,128)S(1)}, f32[2,2,20,20,5]{4,0,3,2,1:T(2,128)}, u32[]{:S(2)}) copy-start(f32[2,2,20,20,5]{4,0,3,2,1:T(2,128)} %get-tuple-element.35) | copy-start | bytes 96004
  586.2 10.1 %collective-permute-start.14 = (f32[2,2,32,6,128]{4,0,3,2,1:T(2,128)S(1)}, f32[2,2,32,6,128]{4,0,3,2,1:T(2,128)S(1)}, u32[]{:S(2)}, u32[]{:S(2)}) collective-permute-start(f32[2,2,32,6,128]{4,0,3,2,1:T(2,128)S(1)} %get-tuple-element.7), channel_id=1, source_target_pairs={{1,0},{2,1},{3,2},{4,3},{5,4},{6,5},{7,6},{8,7},{9,8},{10,9},{11,1... | collective-permute-start | bytes 1179656 | tf_op jit(solution)/shard_map/ppermute | solution.py:27
  588.6 13.0 %collective-permute-start.15 = (f32[2,2,32,6,128]{4,0,3,2,1:T(2,128)S(1)}, f32[2,2,32,6,128]{4,0,3,2,1:T(2,128)S(1)}, u32[]{:S(2)}, u32[]{:S(2)}) collective-permute-start(f32[2,2,32,6,128]{4,0,3,2,1:T(2,128)S(1)} %get-tuple-element.8), channel_id=1, source_target_pairs={{0,1},{1,2},{2,3},{3,4},{4,5},{5,6},{6,7},{7,8},{8,9},{9,10},{10,1... | collective-permute-start | bytes 1179656 | tf_op jit(solution)/shard_map/ppermute | solution.py:24
  (79 other events, 1010.4 us)
where the time goes:
time: 647 us; the launch traced here: 637 us
  blocking collectives  263 us (41%)
  other arithmetic  199 us (31%)
  matrix products  71 us (11%)
  local copies, waits for them, and re-layouts  55.1 us (9%)
  waiting for transfers between devices  29.4 us (5%)
  starting transfers between devices  17.8 us (3%)
    psum x4, blocking collectives, intersections(): cross = lax.psum(cross, ('gx', 'gy')) / ncell  263 us
    another operation x42, other arithmetic, advance(): return jnp.stack([factor * applied[:, 1], -factor * applied[:, 0]], 1)  87.7 us
    add x4, other arithmetic, hamiltonian(): kinetic = -0.5 * lap_term + potential[None, None] * center  83.8 us
    dot_general x4, matrix products, intersections(): lax.dot_general(flat_basis, flat_field, (((1,), (1,)), ((), ())), precisi...  36.9 us
    slice x12, local copies, waits for them, and re-layouts, laplace(): jnp.roll(center, offset, axis=4)  24.3 us
    concatenate x6, other arithmetic, padded_2(): block = jnp.concatenate([low, block, high], axis=dim)  22.7 us
    unnamed x219, local copies, waits for them, and re-layouts  20 us
    ppermute x8, waiting for transfers between devices, padded_2(): lax.ppermute(lax.slice_in_dim(block, block.shape[dim] - width, None, axis...  15.6 us
  transfers between devices with their start and end apart: 16, of which 6 were waited for; matrix products, arithmetic and copies ran while one was open for 18% of the time, Pallas kernels for 0%

commit v1 on v0

v1 whole, which is shorter than its diff:
```python
import functools

import jax
import jax.numpy as jnp
from jax import lax
from jax.experimental import pallas as pl
from jax.experimental.pallas import tpu as pltpu
from jax.sharding import PartitionSpec as P

MESH = pl.DeviceIdType.MESH
coefficients = [
    -5369.0 / 1800.0,
    12.0 / 7.0,
    -15.0 / 56.0,
    10.0 / 189.0,
    -1.0 / 112.0,
    2.0 / 1925.0,
    -1.0 / 16632.0,
]
step_size = 0.25
TERMS = 4
ORBS = 2
KCOL = 8
R = 6


def kernel(sizes, psi_hbm, basis_hbm, pot_hbm, out_hbm, tb, basis, pot, yw, stage, acc, ysend, yrecv, rows, msg, sums,
           load_sem, x_ssem, x_rsem, y_ssem, y_rsem, a_ssem, a_rsem, b_ssem, b_rsem):
    ngx, ngy, ncell = sizes
    width_x, width_y = psi_hbm.shape[2], psi_hbm.shape[3]
    gx, gy = lax.axis_index("gx"), lax.axis_index("gy")
    x_near = [(lax.rem(gx + d, ngx), gy) for d in (ngx - 1, 1)]
    y_near = [(gx, lax.rem(gy + d, ngy)) for d in (ngy - 1, 1)]
    x_peers = [(lax.rem(gx + i, ngx), gy) for i in range(1, ngx)]
    y_peers = [(gx, lax.rem(gy + i, ngy)) for i in range(1, ngy)]

    loads = []
    for j in range(ORBS):
        loads.append(pltpu.make_async_copy(psi_hbm.at[j], tb.at[0, j, :, pl.ds(R, width_x)], load_sem.at[j]))
    loads.append(pltpu.make_async_copy(basis_hbm, basis, load_sem.at[2]))
    loads.append(pltpu.make_async_copy(pot_hbm, pot, load_sem.at[3]))
    for copy in loads:
        copy.start()
    barrier = pltpu.get_barrier_semaphore()
    for peer in x_peers + y_peers:
        pl.semaphore_signal(barrier, inc=1, device_id=peer, device_id_type=MESH)
    rows[...] = jnp.zeros_like(rows)

    pending = []

    def pack(n, j, c, x4, t4):
        base = pl.multiple_of(c * R * width_x + x4 * 4 * R, 8)
        low = ysend.at[n, j, 0, pl.ds(base, 4 * R)]
        high = ysend.at[n, j, 1, pl.ds(base, 4 * R)]
        for i, t in enumerate(t4):
            low[pl.ds(R * i, R), :] = t[0:R]
            high[pl.ds(R * i, R), :] = t[width_y - R:width_y]

    def send(n, j):
        for side in range(2):
            src = R if side == 0 else width_x
            dst = width_x + R if side == 0 else 0
            copy = pltpu.make_async_remote_copy(
                src_ref=ysend.at[n, j, side], dst_ref=yrecv.at[n, j, 1 - side],
                send_sem=y_ssem.at[n, j, side], recv_sem=y_rsem.at[n, j, 1 - side],
                device_id=y_near[side], device_id_type=MESH)
            copy.start()
            pending.append(copy)
            copy = pltpu.make_async_remote_copy(
                src_ref=tb.at[n, j, :, pl.ds(src, R)], dst_ref=tb.at[n, j, :, pl.ds(dst, R)],
                send_sem=x_ssem.at[n, j, side], recv_sem=x_rsem.at[n, j, 1 - side],
                device_id=x_near[side], device_id_type=MESH)
            copy.start()
            pending.append(copy)

    def receive(n, j):
        for side in range(2):
            pltpu.make_async_remote_copy(
                src_ref=ysend.at[n, j, 1 - side], dst_ref=yrecv.at[n, j, side],
                send_sem=y_ssem.at[n, j, 1 - side], recv_sem=y_rsem.at[n, j, side],
                device_id=y_near[side], device_id_type=MESH).wait_recv()
            src = R if side == 1 else width_x
            dst = width_x + R if side == 1 else 0
            pltpu.make_async_remote_copy(
                src_ref=tb.at[n, j, :, pl.ds(src, R)], dst_ref=tb.at[n, j, :, pl.ds(dst, R)],
                send_sem=x_ssem.at[n, j, 1 - side], recv_sem=x_rsem.at[n, j, side],
                device_id=x_near[side], device_id_type=MESH).wait_recv()

        def unpack(x4, carry):
            for c in range(2):
                base = pl.multiple_of(c * R * width_x + x4 * 4 * R, 8)
                low = yrecv.at[n, j, 0, pl.ds(base, 4 * R)]
                high = yrecv.at[n, j, 1, pl.ds(base, 4 * R)]
                for i in range(4):
                    yw[j, c, x4 * 4 + i, pl.ds(8 - R, R), :] = low[pl.ds(R * i, R), :]
                    yw[j, c, x4 * 4 + i, pl.ds(8 + width_y, R), :] = high[pl.ds(R * i, R), :]
            return carry
        lax.fori_loop(0, width_x // 4, unpack, 0)

    def stencil(n, j):
        def body(x, carry):
            potential = pot[x] + (-1.5 * coefficients[0])
            for c in range(2):
                center = tb[n, j, c, x + R]
                total = potential * center
                for k in range(1, R + 1):
                    near = tb[n, j, c, x + R + k] + tb[n, j, c, x + R - k]
                    near = near + (yw[j, c, x, pl.ds(8 + k, width_y), :] + yw[j, c, x, pl.ds(8 - k, width_y), :])
                    near = near + (pltpu.roll(center, k, 1) + pltpu.roll(center, 128 - k, 1))
                    total = total + (-0.5 * coefficients[k]) * near
                stage[j, c, x] = total
            return carry
        lax.fori_loop(0, width_x, body, 0)

    def dots(n):
        for j in range(ORBS):
            for half in range(2):
                ks = range(half * 4, half * 4 + 4)

                def body(x, sums_now):
                    real, imag = tb[n, j, 0, x + R], tb[n, j, 1, x + R]
                    out = []
                    for i, k in enumerate(ks):
                        br, bi = basis[0, k, x], basis[1, k, x]
                        out.append(sums_now[2 * i] + (br * real + bi * imag))
                        out.append(sums_now[2 * i + 1] + (br * imag - bi * real))
                    return tuple(out)
                zero = jnp.zeros((width_y, 128), jnp.float32)
                result = lax.fori_loop(0, width_x, body, (zero,) * 8)
                for i, k in enumerate(ks):
                    rows[pl.ds(16 * j + k, 1), :] = jnp.sum(result[2 * i], axis=0, keepdims=True)
                    rows[pl.ds(16 * j + 8 + k, 1), :] = jnp.sum(result[2 * i + 1], axis=0, keepdims=True)
        ones = jnp.full((8, 128), 1.0 / ncell, jnp.float32)
        line = lax.dot_general(ones, rows[...], (((1,), (1,)), ((), ())), precision=lax.Precision.HIGHEST,
                               preferred_element_type=jnp.float32)
        return line[0:1]

    def reduce_start(n, phase, line):
        peers, ssem, rsem = ((x_peers, a_ssem, a_rsem), (y_peers, b_ssem, b_rsem))[phase]
        msg[n, phase] = line
        copies = []
        for i, peer in enumerate(peers):
            copy = pltpu.make_async_remote_copy(
                src_ref=msg.at[n, phase], dst_ref=sums.at[n, phase, i], send_sem=ssem.at[n, i], recv_sem=rsem.at[n, i],
                device_id=peer, device_id_type=MESH)
            copy.start()
            copies.append(copy)
            pending.append(copy)
        return copies

    def reduce_end(n, phase, copies):
        line = msg[n, phase]
        for i, copy in enumerate(copies):
            copy.wait_recv()
            line = line + sums[n, phase, i]
        return line

    def correct(n, j, line):
        factor = step_size / (n + 1)
        shape = (width_y, 128)
        o_real = [jnp.broadcast_to(line[0:1, 16 * j + k:16 * j + k + 1], shape) for k in range(KCOL)]
        o_imag = [jnp.broadcast_to(line[0:1, 16 * j + 8 + k:16 * j + 9 + k], shape) for k in range(KCOL)]
        last = n == TERMS - 1

        def body(x4, carry):
            packs = ([], [])
            for i in range(4):
                x = x4 * 4 + i
                real, imag = stage[j, 0, x], stage[j, 1, x]
                for k in range(KCOL):
                    br, bi = basis[0, k, x], basis[1, k, x]
                    real = real - (br * o_real[k] - bi * o_imag[k])
                    imag = imag - (br * o_imag[k] + bi * o_real[k])
                t_real, t_imag = factor * imag, -factor * real
                for c, t in ((0, t_real), (1, t_imag)):
                    before = tb[0, j, c, x + R] if n == 0 else acc[j, c, x]
                    acc[j, c, x] = before + t
                    if not last:
                        tb[n + 1, j, c, x + R] = t
                        yw[j, c, x, pl.ds(8, width_y), :] = t
                        packs[c].append(t)
            if not last:
                for c in range(2):
                    pack(n + 1, j, c, x4, packs[c])
            return carry
        lax.fori_loop(0, width_x // 4, body, 0)

    for j in range(ORBS):
        loads[j].wait()

        def first(x4, carry):
            for c in range(2):
                planes = [tb[0, j, c, x4 * 4 + i + R] for i in range(4)]
                for i in range(4):
                    yw[j, c, x4 * 4 + i, pl.ds(8, width_y), :] = planes[i]
                pack(0, j, c, x4, planes)
            return carry
        lax.fori_loop(0, width_x // 4, first, 0)
        if j == 0:
            pl.semaphore_wait(barrier, len(x_peers) + len(y_peers))
        send(0, j)
    loads[2].wait()
    loads[3].wait()
    for n in range(TERMS):
        copies = reduce_start(n, 0, dots(n))
        line = reduce_end(n, 0, copies)
        copies = reduce_start(n, 1, line)
        for j in range(ORBS):
            receive(n, j)
            stencil(n, j)
        line = reduce_end(n, 1, copies)
        for j in range(ORBS):
            correct(n, j, line)
            if n < TERMS - 1:
                send(n + 1, j)
    store = pltpu.make_async_copy(acc, out_hbm, load_sem.at[0])
    store.start()
    for copy in pending:
        copy.wait_send()
    store.wait()


def solution(mesh):
    ngx, ngy = mesh.shape["gx"], mesh.shape["gy"]
    dma = pltpu.SemaphoreType.DMA
    f32 = jnp.float32

    def per_device(psi, basis, potential):
        width_x, width_y, depth = potential.shape
        ncell = width_x * ngx * width_y * ngy * depth
        anywhere = pl.BlockSpec(memory_space=pl.ANY)
        return pl.pallas_call(
            functools.partial(kernel, (ngx, ngy, ncell)),
            out_shape=jax.ShapeDtypeStruct(psi.shape, f32),
            in_specs=[anywhere] * 3,
            out_specs=anywhere,
            scratch_shapes=[
                pltpu.VMEM((TERMS, ORBS, 2, width_x + 2 * R, width_y, depth), f32),
                pltpu.VMEM(basis.shape, f32),
                pltpu.VMEM(potential.shape, f32),
                pltpu.VMEM((ORBS, 2, width_x, 40, depth), f32),
                pltpu.VMEM(psi.shape, f32),
                pltpu.VMEM(psi.shape, f32),
                pltpu.VMEM((TERMS, ORBS, 2, 2 * R * width_x, depth), f32),
                pltpu.VMEM((TERMS, ORBS, 2, 2 * R * width_x, depth), f32),
                pltpu.VMEM((128, depth), f32),
                pltpu.VMEM((TERMS, 2, 1, depth), f32),
                pltpu.VMEM((TERMS, 2, ngy - 1, 1, depth), f32),
                dma((4,)),
                dma((TERMS, ORBS, 2)),
                dma((TERMS, ORBS, 2)),
                dma((TERMS, ORBS, 2)),
                dma((TERMS, ORBS, 2)),
                dma((TERMS, ngx - 1)),
                dma((TERMS, ngx - 1)),
                dma((TERMS, ngy - 1)),
                dma((TERMS, ngy - 1)),
            ],
            compiler_params=pltpu.CompilerParams(
                collective_id=0, has_side_effects=True, vmem_limit_bytes=48 * 2**20),
            name="taylor",
        )(psi, basis, potential)

    placed = (P(None, None, "gx", "gy", None), P(None, None, "gx", "gy", None), P("gx", "gy", None))
    return jax.shard_map(per_device, mesh=mesh, in_specs=placed, out_specs=P(None, None, "gx", "gy", None),
                         check_vma=False)
```

time: 647 us -> 71.1 us (0.11); the launches traced: 637 us -> 71 us
  blocking collectives: 263 us -> 0 us
  other arithmetic: 199 us -> 0 us
  matrix products: 71 us -> 0 us
  Pallas kernels: 0 us -> 65.5 us
  local copies, waits for them, and re-layouts: 55.1 us -> 5.4 us
  waiting for transfers between devices: 29.4 us -> 0 us
  starting transfers between devices: 17.8 us -> 0 us
    psum x4 -> x0, blocking collectives: 263 us -> none  [intersections(): cross = lax.psum(cross, ('gx', 'gy')) / ncell]
    another operation x42 -> x0, other arithmetic: 87.7 us -> none  [advance(): return jnp.stack([factor * applied[:, 1], -factor * applied[:, 0]], 1)]
    add x9 -> x0, other arithmetic: 85.3 us -> none  [the longest x4 83.8 us: hamiltonian(): kinetic = -0.5 * lap_term + potential[None, None] * center]
    dot_general x20 -> x0, matrix products: 71 us -> none  [the longest x4 36.9 us: intersections(): lax.dot_general(flat_basis, flat_field, (((1,), (1,)), ((), ())), precisi...]
    pallas_call x0 -> x1, Pallas kernels: none -> 65.5 us  [per_device(): pl.pallas_call(functools.partial(kernel, (ngx, ngy, ncell)), out_shape=ja...]
    ppermute x16 -> x0, waiting for transfers between devices: 29.4 us -> none  [the longest x8 15.6 us: padded_2(): lax.ppermute(lax.slice_in_dim(block, block.shape[dim] - width, None, axis...]
    slice x14 -> x0, local copies, waits for them, and re-layouts: 25.6 us -> none  [the longest x12 24.3 us: laplace(): jnp.roll(center, offset, axis=4)]
    concatenate x6 -> x0, other arithmetic: 22.7 us -> none  [padded_2(): block = jnp.concatenate([low, block, high], axis=dim)]
  transfers between devices with their start and end apart: 16 -> 0, of which waited for: 6 -> 0; matrix products, arithmetic and copies ran while one was open for 18% -> 0% of each run, Pallas kernels for 0% -> 0%
where the time goes in v1:
time: 71.1 us; the launch traced here: 71 us
  Pallas kernels  65.5 us (92%)
  local copies, waits for them, and re-layouts  5.4 us (8%)
    pallas_call x1, Pallas kernels, per_device(): pl.pallas_call(functools.partial(kernel, (ngx, ngy, ncell)), out_shape=ja...  65.5 us
    unnamed x4, local copies, waits for them, and re-layouts  3.88 us
    pallas_call x1, local copies, waits for them, and re-layouts, per_device(): pl.pallas_call(functools.partial(kernel, (ngx, ngy, ncell)), out_shape=ja...  1.52 us

profile of v1, /device:TPU:1, one launch (start us, length us, event | category | flops | bytes accessed | tf_op | source)
XLA Modules:
  0.0 71.0 jit_solution(3530425613186573027)
XLA Ops:
  0.0 1.2 %copy.4.psi_hbm = f32[2,2,20,20,128]{4,3,2,1,0:T(8,128)S(1)} copy(f32[2,2,20,20,128]{4,1,3,2,0:T(2,128)} %param.3) | data formatting | bytes 1638400 | tf_op args[0]
  1.2 0.0 copy-start
  1.2 2.6 %copy.5.basis_hbm = f32[2,8,20,20,128]{4,3,2,1,0:T(8,128)S(1)} copy(f32[2,8,20,20,128]{4,1,3,2,0:T(8,128)} %param.4) | data formatting | bytes 6553600 | tf_op args[1]
  3.9 0.0 copy-done
  3.9 65.5 %taylor.1 = f32[2,2,20,20,128]{4,3,2,1,0:T(8,128)S(1)} custom-call(f32[2,2,20,20,128]{4,3,2,1,0:T(8,128)S(1)} %copy.4.psi_hbm, f32[2,8,20,20,128]{4,3,2,1,0:T(8,128)S(1)} %copy.5.basis_hbm, f32[20,20,128]{2,1,0:T(8,128)S(1)} %copy-done), custom_call_target="tpu_custom_call" | custom-call | tf_op jit(solution)/shard_map/taylor/pallas_call | solution.py:232
  69.4 1.5 %copy.6 = f32[2,2,20,20,128]{4,1,3,2,0:T(2,128)} copy(f32[2,2,20,20,128]{4,3,2,1,0:T(8,128)S(1)} %taylor.1) | data formatting | bytes 1638400 | tf_op jit(solution)/shard_map/taylor/pallas_call | solution.py:232
Async XLA Ops:
  1.2 2.7 %copy-start = (f32[20,20,128]{2,1,0:T(8,128)S(1)}, f32[20,20,128]{2,1,0:T(8,128)}, u32[]{:S(2)}) copy-start(f32[20,20,128]{2,1,0:T(8,128)} %pot_hbm.1) | copy-start | bytes 614404

commit v2 on v0

v2 whole, which is shorter than its diff:
```python
import functools

import jax
import jax.numpy as jnp
import numpy as np
from jax import lax
from jax.experimental import pallas as pl
from jax.experimental.pallas import tpu as pltpu
from jax.sharding import PartitionSpec as P

MESH = pl.DeviceIdType.MESH
coefficients = [
    -5369.0 / 1800.0,
    12.0 / 7.0,
    -15.0 / 56.0,
    10.0 / 189.0,
    -1.0 / 112.0,
    2.0 / 1925.0,
    -1.0 / 16632.0,
]
step_size = 0.25
TERMS = 4
ORBS = 2
KCOL = 8
R = 6
EDGE = 2 * R
TOP = 16
GROUP = 4


def times_i(tile, even):
    return jnp.where(even, -pltpu.roll(tile, 7, 0), pltpu.roll(tile, 1, 0))


def kernel(sizes, psi_hbm, basis_hbm, pot_hbm, result, tb, basis, columns, pot1, pot, stage, split, circle, ysend, yrecv, rows, msg, sums,
           load_sem, x_ssem, x_rsem, y_ssem, y_rsem, a_ssem, a_rsem, b_ssem, b_rsem):
    ngx, ngy, ncell = sizes
    width_x, width_r = psi_hbm.shape[1], psi_hbm.shape[2]
    width_y = width_r // 2
    tiles = width_r // 8
    gx, gy = lax.axis_index("gx"), lax.axis_index("gy")
    x_near = [(lax.rem(gx + d, ngx), gy) for d in (ngx - 1, 1)]
    y_near = [(gx, lax.rem(gy + d, ngy)) for d in (ngy - 1, 1)]
    core, chip = lax.rem(gx, 2), gx // 2
    cy, cz = gy // 4, lax.rem(gy, 4)
    x_peers = [(chip * 2 + 1 - core, gy)]
    steps = sorted(((i, j, k) for i in range(4) for j in range(4) for k in range(4) if i + j + k > 0),
                   key=lambda step: -sum(min(d, 4 - d) for d in step))
    y_peers = [(lax.rem(chip + i, 4) * 2 + core, lax.rem(cy + j, 4) * 4 + lax.rem(cz + k, 4)) for i, j, k in steps]
    inner = pl.ds(TOP, width_r)
    sublane = lax.broadcasted_iota(jnp.int32, (8, 128), 0)
    lane = lax.broadcasted_iota(jnp.int32, (8, 128), 1)
    even = lax.rem(sublane, 2) == 0

    loads = []
    for j in range(ORBS):
        loads.append(pltpu.make_async_copy(psi_hbm.at[j], tb.at[0, j, pl.ds(R, width_x), inner], load_sem.at[j]))
    for part in range(2):
        loads.append(pltpu.make_async_copy(basis_hbm.at[part], basis.at[:, :, part], load_sem.at[2 + part]))
    loads.append(pltpu.make_async_copy(pot_hbm, pot1, load_sem.at[4]))
    for copy in loads:
        copy.start()
    barrier = pltpu.get_barrier_semaphore()
    outer = (lax.rem(gx + 2 * core + ngx - 1, ngx), gy)
    pl.semaphore_signal(barrier, inc=1, device_id=outer, device_id_type=MESH)
    for peer in x_peers + y_peers:
        pl.semaphore_signal(barrier, inc=1, device_id=peer, device_id_type=MESH)

    pending = []

    def pack(n, j, x2, i, low, high):
        base = pl.multiple_of(x2 * 2 * EDGE, 8)
        for side, (first, second) in ((0, low), (1, high)):
            part = ysend.at[n, j, side, pl.ds(base, 2 * EDGE)]
            part[pl.ds(i * EDGE, first.shape[0]), :] = first
            part[pl.ds(i * EDGE + first.shape[0], second.shape[0]), :] = second

    def x_copy(n, j, side):
        src = R if side == 0 else width_x
        dst = width_x + R if side == 0 else 0
        return pltpu.make_async_remote_copy(
            src_ref=tb.at[n, j, pl.ds(src, R), inner], dst_ref=tb.at[n, j, pl.ds(dst, R), inner],
            send_sem=x_ssem.at[n, j, side], recv_sem=x_rsem.at[n, j, 1 - side],
            device_id=x_near[side], device_id_type=MESH)

    def y_copy(n, j, side):
        return pltpu.make_async_remote_copy(
            src_ref=ysend.at[n, j, side], dst_ref=yrecv.at[n, j, 1 - side],
            send_sem=y_ssem.at[n, j, side], recv_sem=y_rsem.at[n, j, 1 - side],
            device_id=y_near[side], device_id_type=MESH)

    def send(make, n, j):
        for side in range(2):
            copy = make(n, j, side)
            copy.start()
            pending.append(copy)

    def receive(n, j):
        for make in (x_copy, y_copy):
            for side in range(2):
                make(n, j, side).wait_recv()

        def unpack(x2, carry):
            base = pl.multiple_of(x2 * 2 * EDGE, 8)
            for side in range(2):
                part = yrecv.at[n, j, side, pl.ds(base, 2 * EDGE)]
                at = TOP - EDGE if side == 0 else TOP + width_r
                for i in range(2):
                    tb[n, j, R + x2 * 2 + i, pl.ds(at, EDGE), :] = part[pl.ds(i * EDGE, EDGE), :]
            return carry
        lax.fori_loop(0, width_x // 2, unpack, 0)

    def along_z(n, j):
        def halves(x2, carry):
            planes = tb[n, j, pl.ds(R + x2 * 2, 2), inner].reshape(2 * width_r, 128)
            high = planes.astype(jnp.bfloat16)
            at = pl.ds(pl.multiple_of(x2 * 2 * width_r, 16), 2 * width_r)
            split[at, 0:128] = high
            split[at, 128:256] = (planes - high.astype(jnp.float32)).astype(jnp.bfloat16)
            return carry
        lax.fori_loop(0, width_x // 2, halves, 0)
        found = jnp.dot(split[...], circle[...], preferred_element_type=jnp.float32)
        stage[j] = (found[:, 0:128] + found[:, 128:256]).reshape(width_x, width_r, 128)

    def along_xy(n, j):
        half = [-0.5 * c for c in coefficients]

        def body(group, carry):
            x0 = group * GROUP
            for r in range(tiles):
                window = [tb[n, j, x0 + i, pl.ds(TOP + 8 * r, 8), :] for i in range(GROUP + 2 * R)]
                for i in range(GROUP):
                    x = x0 + i
                    total = stage[j, x, pl.ds(8 * r, 8), :] + pot[x, pl.ds(8 * r, 8), :] * window[R + i]
                    for k in range(1, R + 1):
                        near = window[R + i + k] + window[R + i - k]
                        near = near + (tb[n, j, R + x, pl.ds(TOP + 8 * r + 2 * k, 8), :]
                                       + tb[n, j, R + x, pl.ds(TOP + 8 * r - 2 * k, 8), :])
                        total = total + half[k] * near
                    stage[j, x, pl.ds(8 * r, 8), :] = total
            return carry
        lax.fori_loop(0, width_x // GROUP, body, 0)

    def dots(n):
        def body(x, carry):
            out = list(carry)
            for y in range(width_y):
                br, bi = basis[x, y, 0], basis[x, y, 1]
                for j in range(ORBS):
                    real = tb[n, j, R + x, pl.ds(TOP + 2 * y, 1), :]
                    imag = tb[n, j, R + x, pl.ds(TOP + 2 * y + 1, 1), :]
                    at = 4 * (y % 2) + 2 * j
                    out[at] = out[at] + (br * real + bi * imag)
                    out[at + 1] = out[at + 1] + (br * imag - bi * real)
            return tuple(out)
        zero = jnp.zeros((8, 128), jnp.float32)
        found = lax.fori_loop(0, width_x, body, (zero,) * 8)
        packed = jnp.zeros((8, 128), jnp.float32)
        for v in range(4):
            summed = jnp.sum(found[v] + found[4 + v], axis=1, keepdims=True)
            packed = jnp.where(lane == 8 * v + sublane, summed, packed)
        return jnp.sum(packed, axis=0, keepdims=True) * (1.0 / ncell)

    def reduce_start(n, phase, line):
        peers, ssem, rsem = ((x_peers, a_ssem, a_rsem), (y_peers, b_ssem, b_rsem))[phase]
        msg[n, phase] = line
        for i, peer in enumerate(peers):
            pltpu.make_async_remote_copy(
                src_ref=msg.at[n, phase], dst_ref=sums.at[n, phase, i], send_sem=ssem.at[n], recv_sem=rsem.at[n],
                device_id=peer, device_id_type=MESH).start()

    def reduce_wait(n, phase, sem):
        count = len((x_peers, y_peers)[phase])
        every = sums.at[n, phase, pl.ds(0, count)]
        pltpu.make_async_copy(every, every, sem.at[n]).wait()
        return count

    def reduce_end(n, phase):
        count = reduce_wait(n, phase, (a_rsem, b_rsem)[phase])
        parts = [msg[n, phase]] + [sums[n, phase, i] for i in range(count)]
        while len(parts) > 1:
            parts = [sum(parts[i:i + 2][1:], parts[i]) for i in range(0, len(parts), 2)]
        return parts[0]

    def unpack_line(line):
        whole = jnp.broadcast_to(line, (8, 128))
        for v in range(4):
            own = jnp.where(lane == 8 * v + sublane, whole, 0.0)
            rows[pl.ds(8 * v, 8), :] = jnp.broadcast_to(jnp.sum(own, axis=1, keepdims=True), (8, 128))

    def correct(n, j):
        factor = step_size / (n + 1)
        o_real = [jnp.broadcast_to(rows[pl.ds(16 * j + k, 1), :], (8, 128)) for k in range(KCOL)]
        o_imag = [jnp.broadcast_to(rows[pl.ds(16 * j + 8 + k, 1), :], (8, 128)) for k in range(KCOL)]
        last = n == TERMS - 1

        def body(x2, carry):
            for i in range(2):
                x = x2 * 2 + i
                out = []
                for r in range(tiles):
                    along = jnp.zeros((8, 128), jnp.float32)
                    across = jnp.zeros((8, 128), jnp.float32)
                    for k in range(KCOL):
                        column = columns[k, x, pl.ds(8 * r, 8), :]
                        along = along + column * o_real[k]
                        across = across + column * o_imag[k]
                    total = stage[j, x, pl.ds(8 * r, 8), :] - along - times_i(across, even)
                    out.append(factor * total)
                if not last:
                    for r in range(tiles):
                        tb[n + 1, j, R + x, pl.ds(TOP + 8 * r, 8), :] = out[r]
                    pack(n + 1, j, x2, i, (out[0], out[1][0:4]), (out[3][4:8], out[4]))
                else:
                    for r in range(tiles):
                        t = [tb[m, j, R + x, pl.ds(TOP + 8 * r, 8), :] for m in range(TERMS)]
                        result[j, x, pl.ds(8 * r, 8), :] = (t[0] - t[2] + out[r]) - times_i(t[1] - t[3], even)
            return carry
        lax.fori_loop(0, width_x // 2, body, 0)

    offset = lax.rem(lax.broadcasted_iota(jnp.int32, (128, 128), 0) - lax.broadcasted_iota(jnp.int32, (128, 128), 1) + 128, 128)
    high = jnp.zeros((128, 128), jnp.float32)
    low = jnp.zeros((128, 128), jnp.float32)
    for k in range(1, R + 1):
        value = np.float32(-0.5 * coefficients[k])
        first = np.float32(value.astype(jnp.bfloat16))
        here = (offset == k) | (offset == 128 - k)
        high = jnp.where(here, first, high)
        low = jnp.where(here, np.float32(value - first), low)
    for side in range(2):
        circle[pl.ds(128 * side, 128), 0:128] = high.astype(jnp.bfloat16)
        circle[pl.ds(128 * side, 128), 128:256] = low.astype(jnp.bfloat16)

    for j in range(ORBS):
        loads[j].wait()

        def first(x2, carry):
            for i in range(2):
                t = [tb[0, j, R + x2 * 2 + i, pl.ds(TOP + 8 * r, 8), :] for r in (0, 1, 3, 4)]
                pack(0, j, x2, i, (t[0], t[1][0:4]), (t[2][4:8], t[3]))
            return carry
        lax.fori_loop(0, width_x // 2, first, 0)
        if j == 0:
            pl.semaphore_wait(barrier, len(x_peers) + len(y_peers) + 1)
        send(y_copy, 0, j)
        if j == 0:
            send(x_copy, 0, j)
    loads[2].wait()
    loads[3].wait()
    for n in range(TERMS):
        reduce_start(n, 0, dots(n))
        send(x_copy, n, 1)
        if n == 0:
            loads[4].wait()

            def spread(x, carry):
                plane = pot1[x] + (-1.5 * coefficients[0])
                for part in range(2):
                    pot[x, pl.ds(part, width_y, stride=2), :] = plane
                for r in range(tiles):
                    here = basis.at[x, pl.ds(4 * r, 4)].reshape(64, 128)
                    for k in range(KCOL):
                        columns[k, x, pl.ds(8 * r, 8), :] = here[pl.ds(k, 8, stride=8), :]
                return carry
            lax.fori_loop(0, width_x, spread, 0)
        for j in range(ORBS):
            along_z(n, j)
        reduce_start(n, 1, reduce_end(n, 0))
        for j in range(ORBS):
            receive(n, j)
            along_xy(n, j)
        unpack_line(reduce_end(n, 1))
        for j in range(ORBS):
            correct(n, j)
            if n < TERMS - 1:
                send(y_copy, n + 1, j)
                if j == 0:
                    send(x_copy, n + 1, j)
    for copy in pending:
        copy.wait_send()
    for n in range(TERMS):
        reduce_wait(n, 0, a_ssem)
        reduce_wait(n, 1, b_ssem)


def solution(mesh):
    ngx, ngy = mesh.shape["gx"], mesh.shape["gy"]
    dma = pltpu.SemaphoreType.DMA
    f32, bf16 = jnp.float32, jnp.bfloat16

    def per_device(psi, basis, potential):
        width_x, width_y, depth = potential.shape
        ncell = width_x * ngx * width_y * ngy * depth
        far = pl.BlockSpec(memory_space=pltpu.HBM)
        psi = psi.transpose(0, 2, 3, 1, 4).reshape(ORBS, width_x, 2 * width_y, depth)
        basis = basis.transpose(0, 2, 3, 1, 4)
        out = pl.pallas_call(
            functools.partial(kernel, (ngx, ngy, ncell)),
            out_shape=pltpu.VMEM(psi.shape, f32),
            in_specs=[far] * 3,
            out_specs=pl.BlockSpec(memory_space=pltpu.VMEM),
            scratch_shapes=[
                pltpu.VMEM((TERMS, ORBS, width_x + 2 * R, 72, depth), f32),
                pltpu.VMEM((width_x, width_y, 2, KCOL, depth), f32),
                pltpu.VMEM((KCOL, width_x, 2 * width_y, depth), f32),
                pltpu.VMEM((width_x, width_y, depth), f32),
                pltpu.VMEM((width_x, 2 * width_y, depth), f32),
                pltpu.VMEM(psi.shape, f32),
                pltpu.VMEM((2 * width_x * width_y, 2 * depth), bf16),
                pltpu.VMEM((2 * depth, 2 * depth), bf16),
                pltpu.VMEM((TERMS, ORBS, 2, EDGE * width_x, depth), f32),
                pltpu.VMEM((TERMS, ORBS, 2, EDGE * width_x, depth), f32),
                pltpu.VMEM((32, depth), f32),
                pltpu.VMEM((TERMS, 2, 1, depth), f32),
                pltpu.VMEM((TERMS, 2, 63, 1, depth), f32),
                dma((5,)),
                dma((TERMS, ORBS, 2)),
                dma((TERMS, ORBS, 2)),
                dma((TERMS, ORBS, 2)),
                dma((TERMS, ORBS, 2)),
                dma((TERMS,)),
                dma((TERMS,)),
                dma((TERMS,)),
                dma((TERMS,)),
            ],
            compiler_params=pltpu.CompilerParams(
                collective_id=0, has_side_effects=True, vmem_limit_bytes=60 * 2**20),
            name="taylor",
        )(psi, basis, potential)
        return out.reshape(ORBS, width_x, width_y, 2, depth).transpose(0, 3, 1, 2, 4)

    placed = (P(None, None, "gx", "gy", None), P(None, None, "gx", "gy", None), P("gx", "gy", None))
    return jax.shard_map(per_device, mesh=mesh, in_specs=placed, out_specs=P(None, None, "gx", "gy", None),
                         check_vma=False)
```

time: 647 us -> 49.7 us (0.08); the launches traced: 637 us -> 49.4 us
  blocking collectives: 263 us -> 0 us
  other arithmetic: 199 us -> 0 us
  matrix products: 71 us -> 0 us
  local copies, waits for them, and re-layouts: 55.1 us -> 0.89 us
  Pallas kernels: 0 us -> 48.5 us
  waiting for transfers between devices: 29.4 us -> 0 us
  starting transfers between devices: 17.8 us -> 0 us
    psum x4 -> x0, blocking collectives: 263 us -> none  [intersections(): cross = lax.psum(cross, ('gx', 'gy')) / ncell]
    another operation x42 -> x0, other arithmetic: 87.7 us -> none  [advance(): return jnp.stack([factor * applied[:, 1], -factor * applied[:, 0]], 1)]
    add x9 -> x0, other arithmetic: 85.3 us -> none  [the longest x4 83.8 us: hamiltonian(): kinetic = -0.5 * lap_term + potential[None, None] * center]
    dot_general x20 -> x0, matrix products: 71 us -> none  [the longest x4 36.9 us: intersections(): lax.dot_general(flat_basis, flat_field, (((1,), (1,)), ((), ())), precisi...]
    pallas_call x0 -> x1, Pallas kernels: none -> 48.5 us  [per_device(): pl.pallas_call(functools.partial(kernel, (ngx, ngy, ncell)), out_shape=pl...]
    ppermute x16 -> x0, waiting for transfers between devices: 29.4 us -> none  [the longest x8 15.6 us: padded_2(): lax.ppermute(lax.slice_in_dim(block, block.shape[dim] - width, None, axis...]
    slice x14 -> x0, local copies, waits for them, and re-layouts: 25.6 us -> none  [the longest x12 24.3 us: laplace(): jnp.roll(center, offset, axis=4)]
    concatenate x6 -> x0, other arithmetic: 22.7 us -> none  [padded_2(): block = jnp.concatenate([low, block, high], axis=dim)]
  transfers between devices with their start and end apart: 16 -> 0, of which waited for: 6 -> 0; matrix products, arithmetic and copies ran while one was open for 18% -> 0% of each run, Pallas kernels for 0% -> 0%
where the time goes in v2:
time: 49.7 us; the launch traced here: 49.4 us
  Pallas kernels  48.5 us (98%)
  local copies, waits for them, and re-layouts  0.89 us (2%)
    pallas_call x1, Pallas kernels, per_device(): pl.pallas_call(functools.partial(kernel, (ngx, ngy, ncell)), out_shape=pl...  48.5 us

profile of v2, /device:TPU:1, one launch (start us, length us, event | category | flops | bytes accessed | tf_op | source)
XLA Modules:
  0.0 49.4 jit_solution(12928323844210916062)
XLA Ops:
  0.0 48.5 %taylor.1 = f32[2,20,40,128]{3,2,1,0:T(8,128)S(1)} custom-call(f32[2,20,40,128]{3,2,1,0:T(8,128)} %bitcast.9, f32[2,20,20,8,128]{4,3,2,1,0:T(8,128)} %bitcast.8, f32[20,20,128]{2,1,0:T(8,128)} %pot_hbm.1), custom_call_target="tpu_custom_call" | custom-call | tf_op jit(solution)/shard_map/taylor/pallas_call | solution.py:297
  48.5 0.9 %copy.5 = f32[2,2,20,20,128]{4,1,3,2,0:T(2,128)} copy(f32[2,2,20,20,128]{4,1,3,2,0:T(2,128)S(1)} %bitcast.7) | data formatting | bytes 1638400

commit v3 on v2

--- a/solution.py
+++ b/solution.py
@@ -24,6 +24,7 @@
 KCOL = 8
 R = 6
 EDGE = 2 * R
+HALVES = 2
 TOP = 16
 GROUP = 4
 
@@ -83,32 +84,37 @@
             send_sem=x_ssem.at[n, j, side], recv_sem=x_rsem.at[n, j, 1 - side],
             device_id=x_near[side], device_id_type=MESH)
 
-    def y_copy(n, j, side):
+    def y_copy(n, j, side, part):
+        depth = EDGE * width_x // HALVES
+        at = pl.ds(part * depth, depth)
         return pltpu.make_async_remote_copy(
-            src_ref=ysend.at[n, j, side], dst_ref=yrecv.at[n, j, 1 - side],
-            send_sem=y_ssem.at[n, j, side], recv_sem=y_rsem.at[n, j, 1 - side],
+            src_ref=ysend.at[n, j, side, at], dst_ref=yrecv.at[n, j, 1 - side, at],
+            send_sem=y_ssem.at[n, j, side, part], recv_sem=y_rsem.at[n, j, 1 - side, part],
             device_id=y_near[side], device_id_type=MESH)
 
-    def send(make, n, j):
-        for side in range(2):
-            copy = make(n, j, side)
+    def send(make, *key, sides=(0, 1)):
+        for side in sides:
+            copy = make(key[0], key[1], side, *key[2:])
             copy.start()
             pending.append(copy)
 
-    def receive(n, j):
-        for make in (x_copy, y_copy):
-            for side in range(2):
-                make(n, j, side).wait_recv()
+    def receive_x(n, j):
+        for side in range(2):
+            x_copy(n, j, side).wait_recv()
+
+    def receive_y(n, j, part):
+        for side in range(2):
+            y_copy(n, j, side, part).wait_recv()
 
         def unpack(x2, carry):
             base = pl.multiple_of(x2 * 2 * EDGE, 8)
             for side in range(2):
-                part = yrecv.at[n, j, side, pl.ds(base, 2 * EDGE)]
+                rim = yrecv.at[n, j, side, pl.ds(base, 2 * EDGE)]
                 at = TOP - EDGE if side == 0 else TOP + width_r
                 for i in range(2):
-                    tb[n, j, R + x2 * 2 + i, pl.ds(at, EDGE), :] = part[pl.ds(i * EDGE, EDGE), :]
-            return carry
-        lax.fori_loop(0, width_x // 2, unpack, 0)
+                    tb[n, j, R + x2 * 2 + i, pl.ds(at, EDGE), :] = rim[pl.ds(i * EDGE, EDGE), :]
+            return carry
+        lax.fori_loop(part * (width_x // 2 // HALVES), (part + 1) * (width_x // 2 // HALVES), unpack, 0)
 
     def along_z(n, j):
         def halves(x2, carry):
@@ -122,9 +128,9 @@
         found = jnp.dot(split[...], circle[...], preferred_element_type=jnp.float32)
         stage[j] = (found[:, 0:128] + found[:, 128:256]).reshape(width_x, width_r, 128)
 
-    def along_xy(n, j):
-        half = [-0.5 * c for c in coefficients]
-
+    half = [-0.5 * c for c in coefficients]
+
+    def along_x(n, j):
         def body(group, carry):
             x0 = group * GROUP
             for r in range(tiles):
@@ -133,33 +139,43 @@
                     x = x0 + i
                     total = stage[j, x, pl.ds(8 * r, 8), :] + pot[x, pl.ds(8 * r, 8), :] * window[R + i]
                     for k in range(1, R + 1):
-                        near = window[R + i + k] + window[R + i - k]
-                        near = near + (tb[n, j, R + x, pl.ds(TOP + 8 * r + 2 * k, 8), :]
-                                       + tb[n, j, R + x, pl.ds(TOP + 8 * r - 2 * k, 8), :])
-                        total = total + half[k] * near
+                        total = total + half[k] * (window[R + i + k] + window[R + i - k])
                     stage[j, x, pl.ds(8 * r, 8), :] = total
             return carry
         lax.fori_loop(0, width_x // GROUP, body, 0)
 
-    def dots(n):
+    def along_y(n, j, part):
+        def body(x, carry):
+            for r in range(tiles):
+                total = stage[j, x, pl.ds(8 * r, 8), :]
+                for k in range(1, R + 1):
+                    near = tb[n, j, R + x, pl.ds(TOP + 8 * r + 2 * k, 8), :]
+                    near = near + tb[n, j, R + x, pl.ds(TOP + 8 * r - 2 * k, 8), :]
+                    total = total + half[k] * near
+                stage[j, x, pl.ds(8 * r, 8), :] = total
+            return carry
+        lax.fori_loop(part * (width_x // HALVES), (part + 1) * (width_x // HALVES), body, 0, unroll=2)
+
+    def dots(field, j, first_x, first_row, low, high):
         def body(x, carry):
             out = list(carry)
             for y in range(width_y):
                 br, bi = basis[x, y, 0], basis[x, y, 1]
-                for j in range(ORBS):
-                    real = tb[n, j, R + x, pl.ds(TOP + 2 * y, 1), :]
-                    imag = tb[n, j, R + x, pl.ds(TOP + 2 * y + 1, 1), :]
-                    at = 4 * (y % 2) + 2 * j
-                    out[at] = out[at] + (br * real + bi * imag)
-                    out[at + 1] = out[at + 1] + (br * imag - bi * real)
+                real = field[j, first_x + x, pl.ds(first_row + 2 * y, 1), :]
+                imag = field[j, first_x + x, pl.ds(first_row + 2 * y + 1, 1), :]
+                at = 2 * (y % 2)
+                out[at] = out[at] + (br * real + bi * imag)
+                out[at + 1] = out[at + 1] + (br * imag - bi * real)
             return tuple(out)
         zero = jnp.zeros((8, 128), jnp.float32)
-        found = lax.fori_loop(0, width_x, body, (zero,) * 8)
+        found = lax.fori_loop(low, high, body, (zero,) * 4)
+        return [(found[i] + found[2 + i]) * (1.0 / ncell) for i in range(2)]
+
+    def pack_line(vectors):
         packed = jnp.zeros((8, 128), jnp.float32)
-        for v in range(4):
-            summed = jnp.sum(found[v] + found[4 + v], axis=1, keepdims=True)
-            packed = jnp.where(lane == 8 * v + sublane, summed, packed)
-        return jnp.sum(packed, axis=0, keepdims=True) * (1.0 / ncell)
+        for v, vector in enumerate(vectors):
+            packed = jnp.where(lane == 8 * v + sublane, jnp.sum(vector, axis=1, keepdims=True), packed)
+        return jnp.sum(packed, axis=0, keepdims=True)
 
     def reduce_start(n, phase, line):
         peers, ssem, rsem = ((x_peers, a_ssem, a_rsem), (y_peers, b_ssem, b_rsem))[phase]
@@ -188,7 +204,7 @@
             own = jnp.where(lane == 8 * v + sublane, whole, 0.0)
             rows[pl.ds(8 * v, 8), :] = jnp.broadcast_to(jnp.sum(own, axis=1, keepdims=True), (8, 128))
 
-    def correct(n, j):
+    def correct(n, j, part):
         factor = step_size / (n + 1)
         o_real = [jnp.broadcast_to(rows[pl.ds(16 * j + k, 1), :], (8, 128)) for k in range(KCOL)]
         o_imag = [jnp.broadcast_to(rows[pl.ds(16 * j + 8 + k, 1), :], (8, 128)) for k in range(KCOL)]
@@ -213,10 +229,17 @@
                     pack(n + 1, j, x2, i, (out[0], out[1][0:4]), (out[3][4:8], out[4]))
                 else:
                     for r in range(tiles):
-                        t = [tb[m, j, R + x, pl.ds(TOP + 8 * r, 8), :] for m in range(TERMS)]
-                        result[j, x, pl.ds(8 * r, 8), :] = (t[0] - t[2] + out[r]) - times_i(t[1] - t[3], even)
-            return carry
-        lax.fori_loop(0, width_x // 2, body, 0)
+                        result[j, x, pl.ds(8 * r, 8), :] = result[j, x, pl.ds(8 * r, 8), :] + out[r]
+            return carry
+        lax.fori_loop(part * (width_x // 2 // HALVES), (part + 1) * (width_x // 2 // HALVES), body, 0)
+
+    def combine(j):
+        def body(x, carry):
+            for r in range(tiles):
+                t = [tb[m, j, R + x, pl.ds(TOP + 8 * r, 8), :] for m in range(TERMS)]
+                result[j, x, pl.ds(8 * r, 8), :] = (t[0] - t[2]) - times_i(t[1] - t[3], even)
+            return carry
+        lax.fori_loop(0, width_x, body, 0)
 
     offset = lax.rem(lax.broadcasted_iota(jnp.int32, (128, 128), 0) - lax.broadcasted_iota(jnp.int32, (128, 128), 1) + 128, 128)
     high = jnp.zeros((128, 128), jnp.float32)
@@ -242,40 +265,57 @@
         lax.fori_loop(0, width_x // 2, first, 0)
         if j == 0:
             pl.semaphore_wait(barrier, len(x_peers) + len(y_peers) + 1)
-        send(y_copy, 0, j)
+        for part in range(HALVES):
+            send(y_copy, 0, j, part)
         if j == 0:
             send(x_copy, 0, j)
     loads[2].wait()
     loads[3].wait()
+    start = []
+    for j in range(ORBS):
+        start = start + dots(tb.at[0], j, R, TOP, 0, width_x)
+    reduce_start(0, 0, pack_line(start))
+    send(x_copy, 0, 1)
+    loads[4].wait()
+
+    def spread(x, carry):
+        plane = pot1[x] + (-1.5 * coefficients[0])
+        for part in range(2):
+            pot[x, pl.ds(part, width_y, stride=2), :] = plane
+        for r in range(tiles):
+            here = basis.at[x, pl.ds(4 * r, 4)].reshape(64, 128)
+            for k in range(KCOL):
+                columns[k, x, pl.ds(8 * r, 8), :] = here[pl.ds(k, 8, stride=8), :]
+        return carry
+
     for n in range(TERMS):
-        reduce_start(n, 0, dots(n))
-        send(x_copy, n, 1)
+        reduce_start(n, 1, reduce_end(n, 0))
         if n == 0:
-            loads[4].wait()
-
-            def spread(x, carry):
-                plane = pot1[x] + (-1.5 * coefficients[0])
-                for part in range(2):
-                    pot[x, pl.ds(part, width_y, stride=2), :] = plane
-                for r in range(tiles):
-                    here = basis.at[x, pl.ds(4 * r, 4)].reshape(64, 128)
-                    for k in range(KCOL):
-                        columns[k, x, pl.ds(8 * r, 8), :] = here[pl.ds(k, 8, stride=8), :]
-                return carry
             lax.fori_loop(0, width_x, spread, 0)
         for j in range(ORBS):
             along_z(n, j)
-        reduce_start(n, 1, reduce_end(n, 0))
         for j in range(ORBS):
-            receive(n, j)
-            along_xy(n, j)
-        unpack_line(reduce_end(n, 1))
+            receive_x(n, j)
+            along_x(n, j)
+            for part in range(HALVES):
+                receive_y(n, j, part)
+                along_y(n, j, part)
+        if n == TERMS - 1:
+            for j in range(ORBS):
+                combine(j)
+        line = reduce_end(n, 1)
+        unpack_line(line)
         for j in range(ORBS):
-            correct(n, j)
-            if n < TERMS - 1:
-                send(y_copy, n + 1, j)
-                if j == 0:
-                    send(x_copy, n + 1, j)
+            for part in range(HALVES):
+                correct(n, j, part)
+                if n < TERMS - 1:
+                    send(y_copy, n + 1, j, part)
+                    send(x_copy, n + 1, j, sides=(part,))
+        if n < TERMS - 1:
+            start = []
+            for j in range(ORBS):
+                start = start + dots(tb.at[n + 1], j, R, TOP, 0, width_x)
+            reduce_start(n + 1, 0, pack_line(start))
     for copy in pending:
         copy.wait_send()
     for n in range(TERMS):
@@ -316,8 +356,8 @@
                 dma((5,)),
                 dma((TERMS, ORBS, 2)),
                 dma((TERMS, ORBS, 2)),
-                dma((TERMS, ORBS, 2)),
-                dma((TERMS, ORBS, 2)),
+                dma((TERMS, ORBS, 2, HALVES)),
+                dma((TERMS, ORBS, 2, HALVES)),
                 dma((TERMS,)),
                 dma((TERMS,)),
                 dma((TERMS,)),

time: 49.7 us -> 49 us (0.986)
  Pallas kernels: 48.5 us -> 48 us
    pallas_call x1, Pallas kernels: 48.5 us -> 48 us  [per_device(): pl.pallas_call(functools.partial(kernel, (ngx, ngy, ncell)), out_shape=pl...]
where the time goes in v3:
time: 49 us; the launch traced here: 48.9 us
  Pallas kernels  48 us (98%)
  local copies, waits for them, and re-layouts  0.89 us (2%)
    pallas_call x1, Pallas kernels, per_device(): pl.pallas_call(functools.partial(kernel, (ngx, ngy, ncell)), out_shape=pl...  48 us

profile of v3, /device:TPU:1, one launch (start us, length us, event | category | flops | bytes accessed | tf_op | source)
XLA Modules:
  0.0 48.9 jit_solution(9683449165834926562)
XLA Ops:
  0.0 48.0 %taylor.1 = f32[2,20,40,128]{3,2,1,0:T(8,128)S(1)} custom-call(f32[2,20,40,128]{3,2,1,0:T(8,128)} %bitcast.9, f32[2,20,20,8,128]{4,3,2,1,0:T(8,128)} %bitcast.8, f32[20,20,128]{2,1,0:T(8,128)} %pot_hbm.1), custom_call_target="tpu_custom_call" | custom-call | tf_op jit(solution)/shard_map/taylor/pallas_call | solution.py:337
  48.0 0.9 %copy.5 = f32[2,2,20,20,128]{4,1,3,2,0:T(2,128)} copy(f32[2,2,20,20,128]{4,1,3,2,0:T(2,128)S(1)} %bitcast.7) | data formatting | bytes 1638400

commit v4 on v3

--- a/solution.py
+++ b/solution.py
@@ -48,6 +48,12 @@
     steps = sorted(((i, j, k) for i in range(4) for j in range(4) for k in range(4) if i + j + k > 0),
                    key=lambda step: -sum(min(d, 4 - d) for d in step))
     y_peers = [(lax.rem(chip + i, 4) * 2 + core, lax.rem(cy + j, 4) * 4 + lax.rem(cz + k, 4)) for i, j, k in steps]
+    gx_peers = [(lax.rem(gx + i, ngx), gy) for i in range(1, ngx)]
+    gy_peers = [(gx, lax.rem(gy + i, ngy)) for i in sorted(range(1, ngy), key=lambda i: -min(i % 4, 4 - i % 4) - min(i // 4, 4 - i // 4))]
+
+    def peers_of(n, phase):
+        return (gx_peers, gy_peers)[phase] if n == 0 else (x_peers, y_peers)[phase]
+
     inner = pl.ds(TOP, width_r)
     sublane = lax.broadcasted_iota(jnp.int32, (8, 128), 0)
     lane = lax.broadcasted_iota(jnp.int32, (8, 128), 1)
@@ -62,9 +68,7 @@
     for copy in loads:
         copy.start()
     barrier = pltpu.get_barrier_semaphore()
-    outer = (lax.rem(gx + 2 * core + ngx - 1, ngx), gy)
-    pl.semaphore_signal(barrier, inc=1, device_id=outer, device_id_type=MESH)
-    for peer in x_peers + y_peers:
+    for peer in gx_peers + gy_peers:
         pl.semaphore_signal(barrier, inc=1, device_id=peer, device_id_type=MESH)
 
     pending = []
@@ -178,15 +182,15 @@
         return jnp.sum(packed, axis=0, keepdims=True)
 
     def reduce_start(n, phase, line):
-        peers, ssem, rsem = ((x_peers, a_ssem, a_rsem), (y_peers, b_ssem, b_rsem))[phase]
+        ssem, rsem = ((a_ssem, a_rsem), (b_ssem, b_rsem))[phase]
         msg[n, phase] = line
-        for i, peer in enumerate(peers):
+        for i, peer in enumerate(peers_of(n, phase)):
             pltpu.make_async_remote_copy(
                 src_ref=msg.at[n, phase], dst_ref=sums.at[n, phase, i], send_sem=ssem.at[n], recv_sem=rsem.at[n],
                 device_id=peer, device_id_type=MESH).start()
 
     def reduce_wait(n, phase, sem):
-        count = len((x_peers, y_peers)[phase])
+        count = len(peers_of(n, phase))
         every = sums.at[n, phase, pl.ds(0, count)]
         pltpu.make_async_copy(every, every, sem.at[n]).wait()
         return count
@@ -263,19 +267,19 @@
                 pack(0, j, x2, i, (t[0], t[1][0:4]), (t[2][4:8], t[3]))
             return carry
         lax.fori_loop(0, width_x // 2, first, 0)
-        if j == 0:
-            pl.semaphore_wait(barrier, len(x_peers) + len(y_peers) + 1)
-        for part in range(HALVES):
-            send(y_copy, 0, j, part)
-        if j == 0:
-            send(x_copy, 0, j)
     loads[2].wait()
     loads[3].wait()
     start = []
     for j in range(ORBS):
         start = start + dots(tb.at[0], j, R, TOP, 0, width_x)
-    reduce_start(0, 0, pack_line(start))
-    send(x_copy, 0, 1)
+    start = pack_line(start)
+    pl.semaphore_wait(barrier, len(gx_peers) + len(gy_peers))
+    for j in range(ORBS):
+        for part in range(HALVES):
+            send(y_copy, 0, j, part)
+        send(x_copy, 0, j)
+        if j == 0:
+            reduce_start(0, 0, start)
     loads[4].wait()
 
     def spread(x, carry):

time: 49 us -> 47.9 us (0.978)
  Pallas kernels: 48 us -> 46.9 us
    pallas_call x1, Pallas kernels: 48 us -> 46.9 us  [per_device(): pl.pallas_call(functools.partial(kernel, (ngx, ngy, ncell)), out_shape=pl...]
where the time goes in v4:
time: 47.9 us; the launch traced here: 47.8 us
  Pallas kernels  46.9 us (98%)
  local copies, waits for them, and re-layouts  0.89 us (2%)
    pallas_call x1, Pallas kernels, per_device(): pl.pallas_call(functools.partial(kernel, (ngx, ngy, ncell)), out_shape=pl...  46.9 us

profile of v4, /device:TPU:1, one launch (start us, length us, event | category | flops | bytes accessed | tf_op | source)
XLA Modules:
  0.0 47.8 jit_solution(18069310213365910826)
XLA Ops:
  0.0 46.9 %taylor.1 = f32[2,20,40,128]{3,2,1,0:T(8,128)S(1)} custom-call(f32[2,20,40,128]{3,2,1,0:T(8,128)} %bitcast.9, f32[2,20,20,8,128]{4,3,2,1,0:T(8,128)} %bitcast.8, f32[20,20,128]{2,1,0:T(8,128)} %pot_hbm.1), custom_call_target="tpu_custom_call" | custom-call | tf_op jit(solution)/shard_map/taylor/pallas_call | solution.py:341
  46.9 0.9 %copy.5 = f32[2,2,20,20,128]{4,1,3,2,0:T(2,128)} copy(f32[2,2,20,20,128]{4,1,3,2,0:T(2,128)S(1)} %bitcast.7) | data formatting | bytes 1638400

commit v5 on v4

--- a/solution.py
+++ b/solution.py
@@ -293,10 +293,12 @@
         return carry
 
     for n in range(TERMS):
+        if n > 0:
+            along_z(n, 0)
         reduce_start(n, 1, reduce_end(n, 0))
         if n == 0:
             lax.fori_loop(0, width_x, spread, 0)
-        for j in range(ORBS):
+        for j in range(min(n, 1), ORBS):
             along_z(n, j)
         for j in range(ORBS):
             receive_x(n, j)

time: 47.9 us -> 47.9 us (level)
  no operation moved by 1% of the time
where the time goes in v5:
time: 47.9 us; the launch traced here: 47.8 us
  Pallas kernels  46.9 us (98%)
  local copies, waits for them, and re-layouts  0.89 us (2%)
    pallas_call x1, Pallas kernels, per_device(): pl.pallas_call(functools.partial(kernel, (ngx, ngy, ncell)), out_shape=pl...  46.9 us

profile of v5, /device:TPU:1, one launch (start us, length us, event | category | flops | bytes accessed | tf_op | source)
XLA Modules:
  0.0 47.8 jit_solution(12507063797891256930)
XLA Ops:
  0.0 46.9 %taylor.1 = f32[2,20,40,128]{3,2,1,0:T(8,128)S(1)} custom-call(f32[2,20,40,128]{3,2,1,0:T(8,128)} %bitcast.9, f32[2,20,20,8,128]{4,3,2,1,0:T(8,128)} %bitcast.8, f32[20,20,128]{2,1,0:T(8,128)} %pot_hbm.1), custom_call_target="tpu_custom_call" | custom-call | tf_op jit(solution)/shard_map/taylor/pallas_call | solution.py:343
  46.9 0.9 %copy.5 = f32[2,2,20,20,128]{4,1,3,2,0:T(2,128)} copy(f32[2,2,20,20,128]{4,1,3,2,0:T(2,128)S(1)} %bitcast.7) | data formatting | bytes 1638400
